TPU v7x, 32 devices: a whole 2x2x4 slice. The times are simulated.
32 devices in a mesh: dp: 8 (over z, core), tensor: 4 (over y, x).
Axes of the slice: x: 2, y: 2, z: 4, core: 2. Of those that a mesh axis runs over, the one named last changes fastest.
Arguments:
- train_states: bfloat16 [2048, 8192], P('dp'), may hold values from -6 to 6
- qkv_cotangent: bfloat16 [2048, 3072], P('dp', 'tensor'), may hold values from -0.13183594 to 0.13183594
- w_master: float32 [8192, 3072], P('dp', 'tensor'), may hold values from -1.1048543 to 1.1048543
- moment_one: float32 [8192, 3072], P('dp', 'tensor'), may hold values from -1.8 to 1.8
- moment_two: float32 [8192, 3072], P('dp', 'tensor'), may hold values from 0.02 to 2
- prompt_states: bfloat16 [4096, 8192], P('dp'), may hold values from -45 to 45
- norm_gain: float32 [8192], replicated, may hold values from 0.1 to 1.9
- w_out: bfloat16 [2048, 8192], P('tensor'), may hold values from -0.125 to 0.125
Outputs:
- update_dir: float32 [8192, 3072], P('dp', 'tensor')
- prefill_out: bfloat16 [4096, 8192], P(('dp', 'tensor'))
All inputs are finite; a program needn't handle non-finite values.
Results may differ from a plain program's by a relative error of at most 0.02.
Values may be sent and summed in bfloat16 or wider, within the bound.
No kernel may reach another device: no remote copies, remote signals or barrier semaphores. Data moves between devices by JAX's collectives and lax.ppermute only.
A program may use at most 128 MiB of HBM per device.

v0:
```python
import functools

import jax
import jax.numpy as jnp
from jax import lax
from jax.experimental import pallas as pl
from jax.experimental.pallas import tpu as pltpu
from jax.sharding import PartitionSpec as P

HD = 128


beta_one = 0.9
beta_two = 0.95
bias_one = 1.0 - 0.9**8
bias_two = 1.0 - 0.95**8
learn_rate = 0.002
adam_eps = 1e-08
norm_eps = 1e-05
rope_base = 500000.0

MIB = 1024 * 1024
EARLY_BLOCKS = 3


def rope_tables(length, head_size):
    half_width = head_size // 2
    exponent = jnp.arange(half_width, dtype=jnp.float32) * (2.0 / head_size)
    inverse = jnp.power(jnp.float32(rope_base), -exponent)
    position = jnp.arange(length, dtype=jnp.float32)
    angles = position[:, None] * inverse[None, :]
    cosine_table = jnp.concatenate([jnp.cos(angles), jnp.cos(angles)], axis=1)
    sine_table = jnp.concatenate([-jnp.sin(angles), jnp.sin(angles)], axis=1)
    return (cosine_table, sine_table)


def params(mib=16):
    return pltpu.CompilerParams(vmem_limit_bytes=mib * MIB)


def whole_vmem(count):
    return [pl.BlockSpec(memory_space=pltpu.VMEM)] * count


def own_core():
    return lax.rem(lax.axis_index("dp"), 2)


def own_place():
    return lax.div(lax.axis_index("dp"), 2)


def pack_columns(train_states, w_out, rows, line, quarter, early_width):
    width = train_states.shape[1]
    block = early_width // EARLY_BLOCKS

    def kernel(chosen_ref, train_ref, *refs):
        w_out_refs, outs = refs[:EARLY_BLOCKS], refs[EARLY_BLOCKS:]
        place = own_place()
        for distance in range(line):
            for owner in range(2):
                column = pl.multiple_of(((place ^ distance) * 2 + owner) * rows, 128)
                outs[distance][owner] = train_ref[:, pl.ds(column, rows)]
        for entry, w_out_ref in enumerate(w_out_refs):
            outs[line][:, entry * block : (entry + 1) * block] = w_out_ref[...]

    shapes = [jax.ShapeDtypeStruct((2, quarter, rows), train_states.dtype)] * line
    early = jax.ShapeDtypeStruct((w_out.shape[0], early_width), w_out.dtype)
    chosen = jnp.stack([lax.axis_index("tensor"), own_core() * (width // 2 // block)]).astype(jnp.int32)
    outs = pl.pallas_call(
        kernel,
        grid_spec=pltpu.PrefetchScalarGridSpec(
            num_scalar_prefetch=1,
            grid=(1,),
            in_specs=[
                pl.BlockSpec((quarter, width), lambda i, chosen: (chosen[0], 0)),
            ]
            + [
                pl.BlockSpec(
                    (w_out.shape[0], block), lambda i, chosen, entry=entry: (0, chosen[1] + entry)
                )
                for entry in range(EARLY_BLOCKS)
            ],
            out_specs=[pl.BlockSpec(s.shape, lambda i, chosen: (0, 0, 0)) for s in shapes]
            + [pl.BlockSpec(early.shape, lambda i, chosen: (0, 0))],
        ),
        out_shape=shapes + [early],
        compiler_params=params(56),
        name="pack_columns",
    )(chosen, train_states, *([w_out] * EARLY_BLOCKS))
    return outs[:line], outs[line]


def stack_pieces(pieces):
    outer, height, width = pieces[0].shape
    count = len(pieces)

    def kernel(*refs):
        for which in range(outer):
            for i in range(count):
                refs[count + which][i * height : (i + 1) * height] = refs[i][which]

    return pl.pallas_call(
        kernel,
        out_shape=[jax.ShapeDtypeStruct((count * height, width), pieces[0].dtype)] * outer,
        in_specs=whole_vmem(count),
        out_specs=whole_vmem(outer),
        compiler_params=params(),
        name="stack_pieces",
    )(*pieces)


def line_pairs(places):
    return [(2 * a + core, 2 * b + core) for a, b in places for core in range(2)]


def tie(arrays, *others):
    return lax.optimization_barrier((tuple(arrays), others))[0]


class LineGather:
    def __init__(self, block, place, count):
        self.place, self.count = place, count
        self.low, self.high = [block], [block]

    def hop(self, *behind):
        step, count = len(self.low), self.count
        up, down = self.low[-1], self.high[-1]
        if behind:
            up, down = tie((up, down), *behind)
        right = line_pairs([(i, i + 1) for i in range(step - 1, count - 1)])
        left = line_pairs([(i, i - 1) for i in range(1, count - step + 1)])
        if step == count - 1:
            self.high.append(lax.ppermute(down, "dp", left))
            self.low.append(lax.ppermute(up, "dp", right))
            return
        self.low.append(lax.ppermute(up, "dp", right))
        self.high.append(lax.ppermute(down, "dp", left))

    def arrived(self):
        return self.low[-1], self.high[-1]

    def slot(self, step):
        if step == 0:
            return self.place, self.low[0]
        sides = (self.low, self.high)
        choices = line_choice(step, self.place, self.count)
        _, side, entry, owner = choices[-1]
        block = sides[side][entry]
        for holds, side, entry, other in reversed(choices[:-1]):
            block = jnp.where(holds, sides[side][entry], block)
            owner = jnp.where(holds, other, owner)
        return owner, block


def line_choice(step, place, count):
    is_low, is_high = place >= step, place <= count - 1 - step
    spare = count - step
    return [
        (is_low, 0, step, place - step),
        (jnp.logical_and(jnp.logical_not(is_low), is_high), 1, step, place + step),
        (
            jnp.logical_and(jnp.logical_not(is_low), jnp.logical_not(is_high)),
            1,
            spare,
            place + spare,
        ),
    ][: 2 if 2 * step <= count else 3]


def place_cotangents(blocks, n_tensor):
    tokens, width = blocks[0].shape
    quarter = tokens // n_tensor
    count = len(blocks)

    def kernel(*refs):
        for distance in range(count):
            refs[count][:, distance * quarter : (distance + 1) * quarter] = refs[distance][...]

    return pl.pallas_call(
        kernel,
        out_shape=jax.ShapeDtypeStruct((n_tensor, count * quarter, width), blocks[0].dtype),
        in_specs=whole_vmem(count),
        out_specs=pl.BlockSpec(memory_space=pltpu.VMEM),
        compiler_params=params(),
        name="place_cotangents",
    )(*[block.reshape(n_tensor, quarter, width) for block in blocks])


def plane_permute(block, count, distance):
    return lax.ppermute(block, "tensor", [(j, j ^ distance) for j in range(count)])


class PlaneGather:
    def __init__(self, pair, count):
        self.count = count
        if count != 4:
            own = lax.axis_index("tensor")
            gathered = [lax.all_gather(block, "tensor", axis=0) for block in pair]
            self.blocks = [
                [lax.dynamic_index_in_dim(g, own ^ b, 0, keepdims=False) for g in gathered]
                for b in range(count)
            ]
            return
        one, two = [None, None], [None, None]
        for owner in range(2):
            one[owner] = plane_permute(pair[owner], count, 1)
            two[1 - owner] = plane_permute(pair[1 - owner], count, 2)
        self.blocks = [list(pair), one, two]

    def passed(self):
        return [self.blocks[1][0], self.blocks[2][1]]

    def second(self, *behind):
        if self.count == 4:
            up, down = tie(self.passed(), *behind)
            self.blocks.append(
                [plane_permute(up, self.count, 2), plane_permute(down, self.count, 1)]
            )


def gradient_term(blocks, cotangents, sibling):
    n_tensor, depth, width = cotangents.shape
    size = blocks[0][0].shape[1]
    flat = [block for pair in blocks for block in pair]

    def kernel(*refs):
        cotangent_ref, out_ref = refs[len(flat) :]
        index = lax.axis_index("tensor")
        owner = 1 - own_core() if sibling else own_core()
        total = None
        for distance in range(n_tensor):
            lower, upper = refs[2 * distance : 2 * distance + 2]
            product = lax.dot_general(
                jnp.where(owner == 0, lower[...], upper[...]),
                cotangent_ref[index ^ distance],
                (((0,), (0,)), ((), ())),
                preferred_element_type=jnp.float32,
            )
            total = product if total is None else total + product
        out_ref[...] = total.astype(out_ref.dtype)

    return pl.pallas_call(
        kernel,
        out_shape=jax.ShapeDtypeStruct((size, width), jnp.bfloat16 if sibling else jnp.float32),
        in_specs=whole_vmem(len(flat) + 1),
        out_specs=pl.BlockSpec(memory_space=pltpu.VMEM),
        compiler_params=params(28),
        cost_estimate=pl.CostEstimate(
            flops=2 * n_tensor * depth * size * width,
            bytes_accessed=n_tensor * depth * (4 * size + 2 * width) + 4 * size * width,
            transcendentals=0,
        ),
        name="gradient_term",
    )(*flat, cotangents)


def adam_rows(kept, got, w_master, moment_one, moment_two):
    rows, width = kept.shape
    tile = min(128, rows)

    def kernel(kept_ref, got_ref, master_ref, one_ref, two_ref, update_ref, weight_ref):
        gradient = kept_ref[...] + got_ref[...].astype(jnp.float32)
        moment_new = beta_one * one_ref[...] + (1.0 - beta_one) * gradient
        second_new = beta_two * two_ref[...] + (1.0 - beta_two) * gradient * gradient
        scaled = second_new * (1.0 / bias_two)
        update = moment_new * (1.0 / bias_one) / (scaled * lax.rsqrt(scaled) + adam_eps)
        update_ref[...] = update
        weight_ref[...] = (master_ref[...] - learn_rate * update).astype(weight_ref.dtype)

    here = pl.BlockSpec((tile, width), lambda i: (i, 0))
    return pl.pallas_call(
        kernel,
        grid=(rows // tile,),
        out_shape=[
            jax.ShapeDtypeStruct((rows, width), jnp.float32),
            jax.ShapeDtypeStruct((rows, width), jnp.bfloat16),
        ],
        in_specs=[here] * 5,
        out_specs=[here] * 2,
        compiler_params=params(),
        cost_estimate=pl.CostEstimate(
            flops=16 * rows * width, bytes_accessed=24 * rows * width, transcendentals=rows * width
        ),
        name="adam_rows",
    )(kept, got, w_master, moment_one, moment_two)


def norm_columns(states, gain, rows, line):
    length, width = states.shape
    tile = 64

    def kernel(states_ref, gain_ref, kept, sent):
        core = own_core()
        total = jnp.zeros((tile, 1), jnp.float32)
        for block in range(2 * line):
            piece = states_ref[:, block * rows : (block + 1) * rows].astype(jnp.float32)
            total = total + jnp.sum(piece * piece, axis=1, keepdims=True)
        scale = lax.rsqrt(total / width + norm_eps)
        for flag in range(2):

            @pl.when(core == flag)
            def _():
                for block in range(2 * line):
                    out = kept if block % 2 == flag else sent
                    columns = slice(block * rows, (block + 1) * rows)
                    piece = states_ref[:, columns].astype(jnp.float32)
                    out[block // 2] = (piece * scale * gain_ref[:, columns]).astype(out.dtype)

    return pl.pallas_call(
        kernel,
        grid=(length // tile,),
        out_shape=[jax.ShapeDtypeStruct((line, length, rows), jnp.bfloat16)] * 2,
        in_specs=[
            pl.BlockSpec((tile, width), lambda i: (i, 0)),
            pl.BlockSpec((1, width), lambda i: (0, 0)),
        ],
        out_specs=[pl.BlockSpec((line, tile, rows), lambda i: (0, i, 0))] * 2,
        compiler_params=params(),
        cost_estimate=pl.CostEstimate(
            flops=6 * length * width, bytes_accessed=4 * length * width, transcendentals=0
        ),
        name="norm_columns",
    )(states, gain.reshape(1, width))


def accumulate(totals, states, slots, dtypes):
    _, length, depth = states[0].shape
    sides = len(states)
    width = slots[0][1].shape[1]
    count = len(slots)
    tile = min(256, length)
    owners = jnp.stack([jnp.asarray(owner, jnp.int32) for owner, _ in slots])
    weights = [weight for _, weight in slots]

    def kernel(owners_ref, *refs):
        weight_refs = refs[sides * count : (sides + 1) * count]
        for side, out_ref in enumerate(refs[-sides:]):
            result = None if totals is None else refs[(sides + 1) * count + side][...]
            for slot in range(count):
                product = jnp.dot(
                    refs[side * count + slot][0],
                    weight_refs[slot][...],
                    preferred_element_type=jnp.float32,
                )
                result = product if result is None else result + product
            out_ref[...] = result.astype(out_ref.dtype)

    def state_spec(slot):
        return pl.BlockSpec((1, tile, depth), lambda i, chosen: (chosen[slot], i, 0))

    before = list(totals or [])
    row_spec = pl.BlockSpec((tile, width), lambda i, chosen: (i, 0))
    return pl.pallas_call(
        kernel,
        grid_spec=pltpu.PrefetchScalarGridSpec(
            num_scalar_prefetch=1,
            grid=(length // tile,),
            in_specs=[state_spec(slot) for slot in range(count)] * sides
            + [pl.BlockSpec((depth, width), lambda i, chosen: (0, 0))] * count
            + [row_spec] * len(before),
            out_specs=[row_spec] * sides,
        ),
        out_shape=[jax.ShapeDtypeStruct((length, width), dtype) for dtype in dtypes],
        compiler_params=params(20),
        cost_estimate=pl.CostEstimate(
            flops=2 * sides * count * length * depth * width,
            bytes_accessed=2 * count * depth * (2 * length + width) + 16 * length * width,
            transcendentals=0,
        ),
        name="accumulate",
    )(owners, *[array for array in states for _ in range(count)], *weights, *before)


def attention(kept, got, cosine_table, sine_table):
    length, width = kept.shape
    heads = width // HD - 2
    tile = min(128, length)

    def rope(u, cosine, sine):
        return u * cosine + pltpu.roll(u, HD // 2, 1) * sine

    def kernel(kept_ref, got_ref, cos_ref, sin_ref, out_ref):
        def columns(index, here=slice(None)):
            there = slice(index * HD, (index + 1) * HD)
            return kept_ref[here, there] + got_ref[here, there].astype(jnp.float32)

        keys = rope(columns(heads), cos_ref[...], sin_ref[...]).astype(jnp.bfloat16)
        values = columns(heads + 1).astype(jnp.bfloat16)
        for begin in range(0, length, tile):
            here, upto = slice(begin, begin + tile), begin + tile
            row = lax.broadcasted_iota(jnp.int32, (tile, upto), 0) + begin
            seen = row >= lax.broadcasted_iota(jnp.int32, (tile, upto), 1)
            for head in range(heads):
                query = rope(columns(head, here), cos_ref[here], sin_ref[here])
                query = (query * HD**-0.5).astype(jnp.bfloat16)
                scores = lax.dot_general(
                    query,
                    keys[:upto],
                    (((1,), (1,)), ((), ())),
                    preferred_element_type=jnp.float32,
                )
                scores = jnp.where(seen, scores, -jnp.inf)
                raised = jnp.exp(scores - jnp.max(scores, axis=1, keepdims=True))
                weights = raised * (1.0 / jnp.sum(raised, axis=1, keepdims=True))
                out_ref[here, head * HD : (head + 1) * HD] = jnp.dot(
                    weights.astype(jnp.bfloat16), values[:upto], preferred_element_type=jnp.float32
                ).astype(jnp.bfloat16)

    return pl.pallas_call(
        kernel,
        out_shape=jax.ShapeDtypeStruct((length, heads * HD), jnp.bfloat16),
        in_specs=whole_vmem(4),
        out_specs=pl.BlockSpec(memory_space=pltpu.VMEM),
        compiler_params=params(10),
        cost_estimate=pl.CostEstimate(
            flops=4 * heads * length * length * HD,
            bytes_accessed=9 * length * width,
            transcendentals=heads * length * length,
        ),
        name="attention",
    )(kept, got, cosine_table, sine_table)


def by_source(mine, other, n_tensor):
    kept, depth = mine.shape[0] // n_tensor, mine.shape[1]

    def kernel(mine_ref, other_ref, out_ref):
        index = lax.axis_index("tensor")
        for distance in range(n_tensor):
            columns = pl.ds(pl.multiple_of((index ^ distance) * depth, depth), depth)
            rows = slice(distance * kept, (distance + 1) * kept)
            out_ref[:kept, columns] = mine_ref[rows]
            out_ref[kept:, columns] = other_ref[rows]

    return pl.pallas_call(
        kernel,
        out_shape=jax.ShapeDtypeStruct((2 * kept, n_tensor * depth), mine.dtype),
        in_specs=whole_vmem(2),
        out_specs=pl.BlockSpec(memory_space=pltpu.VMEM),
        compiler_params=params(),
        name="by_source",
    )(mine, other)


def fetch(*arrays):
    parts = 4
    if sum(a.size * a.dtype.itemsize for a in arrays) > 20 * MIB:
        return arrays

    def kernel(*refs):
        sems = refs[-1]
        copies = []
        for which in range(len(arrays)):
            rows = arrays[which].shape[0] // parts
            for part in range(parts):
                here = pl.ds(part * rows, rows)
                copies.append(
                    pltpu.make_async_copy(
                        refs[which].at[here],
                        refs[len(arrays) + which].at[here],
                        sems.at[which * parts + part],
                    )
                )
        for copy in copies:
            copy.start()
        for copy in copies:
            copy.wait()

    return pl.pallas_call(
        kernel,
        out_shape=[jax.ShapeDtypeStruct(a.shape, a.dtype) for a in arrays],
        in_specs=[pl.BlockSpec(memory_space=pl.ANY)] * len(arrays),
        out_specs=whole_vmem(len(arrays)),
        scratch_shapes=[pltpu.SemaphoreType.DMA((parts * len(arrays),))],
        compiler_params=params(24),
        cost_estimate=pl.CostEstimate(
            flops=0, bytes_accessed=2 * sum(a.size * 2 for a in arrays), transcendentals=0
        ),
        name="fetch",
    )(*arrays)


def lay_out(blocks):
    kept = blocks[0][0].shape[0]
    half = sum(block.shape[1] for block in blocks[0])

    def kernel(*refs):
        out_ref = refs[-1]
        core = own_core()
        for flag in range(2):

            @pl.when(core == flag)
            def _():
                entry = 0
                for side in range(2):
                    begin = (flag ^ side) * half
                    for block in blocks[side]:
                        stop = begin + block.shape[1]
                        out_ref[:, begin:stop] = refs[entry][...]
                        begin, entry = stop, entry + 1

    flat = [block for side in blocks for block in side]
    return pl.pallas_call(
        kernel,
        out_shape=jax.ShapeDtypeStruct((kept, 2 * half), flat[0].dtype),
        in_specs=whole_vmem(len(flat)),
        out_specs=pl.BlockSpec(memory_space=pltpu.VMEM),
        compiler_params=params(),
        name="lay_out",
    )(*flat)


def body(
    train_states, qkv_cotangent, w_master, moment_one, moment_two, prompt_states, norm_gain, w_out
):
    n_dp = lax.axis_size("dp")
    n_tensor = lax.axis_size("tensor")
    line = n_dp // 2
    tensor_index = lax.axis_index("tensor")
    core, place = own_core(), own_place()
    siblings = [(i, i ^ 1) for i in range(n_dp)]
    rows, slice_width = w_master.shape
    tokens, width = train_states.shape
    length = prompt_states.shape[0]
    query_width = slice_width - 2 * HD

    kept_states, sent_states = norm_columns(prompt_states, norm_gain, rows, line)
    got_states = lax.ppermute(sent_states, "dp", siblings)

    core_width = width // 2
    early_width = EARLY_BLOCKS * core_width // 32
    packed, w_early = pack_columns(
        train_states, w_out, rows, line, tokens // n_tensor, early_width
    )
    def across(block, distance):
        return lax.ppermute(block, "dp", line_pairs([(i, i ^ distance) for i in range(line)]))

    pieces = [packed[0]] + [across(packed[distance], distance) for distance in range(1, line)]
    pieces = tie(pieces, kept_states)

    cotangents = [qkv_cotangent, across(qkv_cotangent, 1)]
    spread = PlaneGather(stack_pieces(pieces), n_tensor)
    behind = pieces
    for distance in range(2, line):
        cotangents.append(across(tie((qkv_cotangent,), *behind)[0], distance))
        behind = cotangents[-1:]
    spread.second(cotangents[2], spread.blocks[1:])
    all_cotangents = place_cotangents(cotangents, n_tensor)

    w_rest = lax.dynamic_slice(
        w_out,
        (0, core * core_width + early_width),
        (w_out.shape[0], core_width - early_width),
    )
    early_weight = lax.all_gather(w_early, "tensor", axis=0, tiled=True)
    (w_rest,) = tie((w_rest,), spread.blocks, cotangents, early_weight)
    rest_weight = lax.all_gather(w_rest, "tensor", axis=0, tiled=True)

    sent = gradient_term(spread.blocks, all_cotangents, True)
    got = lax.ppermute(sent, "dp", siblings)
    kept = gradient_term(spread.blocks, all_cotangents, False)
    update_dir, weight = adam_rows(kept, got, w_master, moment_one, moment_two)

    weights = LineGather(weight, place, line)

    def add(totals, states, steps, dtype=jnp.float32):
        slots = [weights.slot(step) for step in steps]
        return accumulate(totals, states, slots, [dtype] * len(states))

    both_states = (kept_states, got_states)
    for _ in range(1, line - 1):
        weights.hop()
    totals = add(None, both_states, range(line - 2))
    cosine_table, sine_table = rope_tables(length, HD)
    cosine_table, sine_table, *totals = tie((cosine_table, sine_table, *totals))
    weights.hop(*totals, cosine_table, sine_table)
    own_total, other_total = add(totals, both_states, [line - 2])
    (other_total,) = add([other_total], [got_states], [line - 1], jnp.bfloat16)
    got_total = lax.ppermute(other_total, "dp", siblings)
    (own_total,) = add([own_total], [kept_states], [line - 1])
    attended = attention(own_total, got_total, cosine_table, sine_table)

    kept_rows = length // n_tensor
    heads = []
    for distance in range(n_tensor):
        target = tensor_index ^ distance
        block = lax.dynamic_slice(attended, (target * kept_rows, 0), (kept_rows, query_width))
        if distance:
            block = lax.ppermute(block, "tensor", [(j, j ^ distance) for j in range(n_tensor)])
        heads.append(block)
    fetched = fetch(early_weight, rest_weight)
    heads = tie(heads, *fetched)
    (mine,) = stack_pieces([head[None] for head in heads])
    other = lax.ppermute(mine, "dp", siblings)
    both = by_source(mine, other, n_tensor)
    mine, sent = [], []
    for weight in fetched:
        made = jnp.dot(both, weight, preferred_element_type=jnp.float32).astype(jnp.bfloat16)
        mine.append(made[:kept_rows])
        sent.append(made[kept_rows:])
    summed = lay_out((mine, [lax.ppermute(rows, "dp", siblings) for rows in sent]))
    return (update_dir, summed)


def solution(mesh):
    placed = (
        P("dp", None),
        P("dp", "tensor"),
        P("dp", "tensor"),
        P("dp", "tensor"),
        P("dp", "tensor"),
        P("dp", None),
        P(),
        P("tensor", None),
    )
    return jax.shard_map(
        body,
        mesh=mesh,
        in_specs=placed,
        out_specs=(P("dp", "tensor"), P(("dp", "tensor"), None)),
        check_vma=False,
    )
```

profile of v0, /device:TPU:0, one launch (start us, length us, event | category | flops | bytes accessed | tf_op | source)
XLA Modules:
  0.0 255.7 jit_solution(12869396784066921870)
XLA Ops:
  7.8 3.4 %pack_columns.1 = (bf16[2,64,1024]{2,1,0:T(8,128)(2,1)}, bf16[2,64,1024]{2,1,0:T(8,128)(2,1)}, bf16[2,64,1024]{2,1,0:T(8,128)(2,1)}, bf16[2,64,1024]{2,1,0:T(8,128)(2,1)}, bf16[512,384]{1,0:T(8,128)(2,1)}) custom-call(s32[2]{0:T(128)} %pad_add_fusion.chosen_ref, bf16[256,8192]{1,0:T(8,128)(2,1)} %train_ref.1, bf16[512,8192]{1,0:T(8,128)(2,1)} %refs_2_.1, ...), custom_call_target="tpu_custom_call" | custom-call | tf_op jit(solution)/shard_map/pack_columns/pallas_call | solution.py:70
  11.3 3.1 %collective-permute-start = (bf16[2,64,1024]{2,1,0:T(8,128)(2,1)}, bf16[2,64,1024]{2,1,0:T(8,128)(2,1)S(1)}, u32[]{:S(2)}, u32[]{:S(2)}) collective-permute-start(bf16[2,64,1024]{2,1,0:T(8,128)(2,1)} %get-tuple-element.39), channel_id=1, source_target_pairs={{0,8},{4,12},{8,0},{12,4},{16,24},{20,28},{24,16},{28,20},{1,9},{5... | collective-permute-start | bytes 786440 | tf_op jit(solution)/shard_map/ppermute | solution.py:537
  16.9 3.4 %copy-done.4 = bf16[512,8192]{1,0:T(8,128)(2,1)S(1)} copy-done((bf16[512,8192]{1,0:T(8,128)(2,1)S(1)}, bf16[512,8192]{1,0:T(8,128)(2,1)}, u32[]{:S(2)}) %copy-start.4) | copy-done | bytes 8388632
  20.3 6.0 %norm_columns.1 = (bf16[4,512,1024]{2,1,0:T(8,128)(2,1)S(1)}, bf16[4,512,1024]{2,1,0:T(8,128)(2,1)}) custom-call(bf16[512,8192]{1,0:T(8,128)(2,1)S(1)} %copy-done.4, f32[1,8192]{1,0:T(1,128)S(1)} %bitcast.24), custom_call_target="tpu_custom_call" | custom-call | flops 25165824 | bytes 16777216 | tf_op jit(solution)/shard_map/norm_columns/pallas_call | solution.py:310
  28.3 7.7 %collective-permute-done.1.refs_2_ = bf16[2,64,1024]{2,1,0:T(8,128)(2,1)S(1)} collective-permute-done((bf16[2,64,1024]{2,1,0:T(8,128)(2,1)}, bf16[2,64,1024]{2,1,0:T(8,128)(2,1)S(1)}, u32[]{:S(2)}, u32[]{:S(2)}) %collective-permute-start.1) | collective-permute-done | bytes 262176 | tf_op jit(solution)/shard_map/ppermute | solution.py:537
  40.1 5.8 %collective-permute-start.7 = (bf16[256,768]{1,0:T(8,128)(2,1)S(1)}, bf16[256,768]{1,0:T(8,128)(2,1)}, u32[]{:S(2)}, u32[]{:S(2)}) collective-permute-start(bf16[256,768]{1,0:T(8,128)(2,1)S(1)} %copy-done.14), channel_id=1, source_target_pairs={{0,16},{4,20},{8,24},{12,28},{16,0},{20,4},{24,8},{28,12},{1,17},{... | collective-permute-start | bytes 1179656 | tf_op jit(solution)/shard_map/ppermute | solution.py:537
  45.9 15.5 %collective-permute-done.7 = bf16[256,768]{1,0:T(8,128)(2,1)} collective-permute-done((bf16[256,768]{1,0:T(8,128)(2,1)S(1)}, bf16[256,768]{1,0:T(8,128)(2,1)}, u32[]{:S(2)}, u32[]{:S(2)}) %collective-permute-start.7) | collective-permute-done | bytes 393248 | tf_op jit(solution)/shard_map/ppermute | solution.py:537
  62.7 4.2 %collective-permute-done.4.refs_3_ = bf16[256,1024]{1,0:T(8,128)(2,1)S(1)} collective-permute-done((bf16[256,1024]{1,0:T(8,128)(2,1)S(1)}, bf16[256,1024]{1,0:T(8,128)(2,1)S(1)}, u32[]{:S(2)}, u32[]{:S(2)}) %collective-permute-start.4) | collective-permute-done | bytes 524320 | tf_op jit(solution)/shard_map/ppermute | solution.py:191
  69.2 4.2 %constant_dynamic-slice_fusion = bf16[512,3712]{1,0:T(8,128)(2,1)} fusion(bf16[512,8192]{1,0:T(8,128)(2,1)} %refs_2_.1, s32[]{:T(128)S(6)} %select_n.76), kind=kLoop, calls=%fused_computation.11 | loop fusion | bytes 7602180 | tf_op jit(solution)/shard_map/dynamic_slice | solution.py:551
  73.4 6.4 %collective-permute-done.10 = bf16[256,768]{1,0:T(8,128)(2,1)} collective-permute-done((bf16[256,768]{1,0:T(8,128)(2,1)S(1)}, bf16[256,768]{1,0:T(8,128)(2,1)}, u32[]{:S(2)}, u32[]{:S(2)}) %collective-permute-start.10) | collective-permute-done | bytes 393248 | tf_op jit(solution)/shard_map/ppermute | solution.py:537
  82.4 3.5 %gradient_term.3 = bf16[1024,768]{1,0:T(8,128)(2,1)S(1)} custom-call(bf16[256,1024]{1,0:T(8,128)(2,1)S(1)} %get-tuple-element.47.refs_0_, bf16[256,1024]{1,0:T(8,128)(2,1)S(1)} %get-tuple-element.48.refs_1_, bf16[256,1024]{1,0:T(8,128)(2,1)S(1)} %collective-permute-done.3.refs_2_, bf16[256,1024]{1,0:T(8,128)(2,1)S(1)} %collective-permute-done.4.refs_3_, ...), custom_call_target="tpu_custom_call" | custom-call | flops 1610612736 | bytes 8912896 | tf_op jit(solution)/shard_map/gradient_term/pallas_call | solution.py:243
  86.5 3.7 %gradient_term.2.kept_ref = f32[1024,768]{1,0:T(8,128)S(1)} custom-call(bf16[256,1024]{1,0:T(8,128)(2,1)S(1)} %get-tuple-element.47.refs_0_, bf16[256,1024]{1,0:T(8,128)(2,1)S(1)} %get-tuple-element.48.refs_1_, bf16[256,1024]{1,0:T(8,128)(2,1)S(1)} %collective-permute-done.3.refs_2_, bf16[256,1024]{1,0:T(8,128)(2,1)S(1)} %collective-permute-done.4.refs_3_, ...), custom_call_target="tpu_custom_call" | custom-call | flops 1610612736 | bytes 8912896 | tf_op jit(solution)/shard_map/gradient_term/pallas_call | solution.py:243
  91.3 4.2 %adam_rows.1 = (f32[1024,768]{1,0:T(8,128)}, bf16[1024,768]{1,0:T(8,128)(2,1)S(1)}) custom-call(f32[1024,768]{1,0:T(8,128)S(1)} %gradient_term.2.kept_ref, bf16[1024,768]{1,0:T(8,128)(2,1)S(1)} %collective-permute-done.12.got_ref, f32[1024,768]{1,0:T(8,128)S(1)} %copy-done.5, f32[1024,768]{1,0:T(8,128)S(1)} %copy-done.6, f32[1024,768]{1,0:T(8,128)S(1)} %copy-done.7), custom_call_target="tpu_custom_call" | custom-call | flops 12582912 | bytes 18874368 | tf_op jit(solution)/shard_map/adam_rows/pallas_call | solution.py:272
  95.5 5.4 %collective-permute-start.13 = (bf16[1024,768]{1,0:T(8,128)(2,1)S(1)}, bf16[1024,768]{1,0:T(8,128)(2,1)}, u32[]{:S(2)}, u32[]{:S(2)}) collective-permute-start(bf16[1024,768]{1,0:T(8,128)(2,1)S(1)} %get-tuple-element.54.refs_4_), channel_id=1, source_target_pairs={{0,8},{4,12},{8,16},{12,20},{16,24},{20,28},{1,9},{5,13},{9,17},{1... | collective-permute-start | bytes 4718600 | tf_op jit(solution)/shard_map/ppermute | solution.py:137
  102.1 31.4 %collective-permute-done.13 = bf16[1024,768]{1,0:T(8,128)(2,1)} collective-permute-done((bf16[1024,768]{1,0:T(8,128)(2,1)S(1)}, bf16[1024,768]{1,0:T(8,128)(2,1)}, u32[]{:S(2)}, u32[]{:S(2)}) %collective-permute-start.13) | collective-permute-done | bytes 1572896 | tf_op jit(solution)/shard_map/ppermute | solution.py:137
  135.4 3.4 %collective-permute-done.15 = bf16[1024,768]{1,0:T(8,128)(2,1)S(1)} collective-permute-done((bf16[1024,768]{1,0:T(8,128)(2,1)S(1)}, bf16[1024,768]{1,0:T(8,128)(2,1)S(1)}, u32[]{:S(2)}, u32[]{:S(2)}) %collective-permute-start.15) | collective-permute-done | bytes 1572896 | tf_op jit(solution)/shard_map/ppermute | solution.py:138
  142.3 3.3 %copy-done.1 = bf16[4,512,1024]{2,1,0:T(8,128)(2,1)S(1)} copy-done((bf16[4,512,1024]{2,1,0:T(8,128)(2,1)S(1)}, bf16[4,512,1024]{2,1,0:T(8,128)(2,1)}, u32[]{:S(2)}) %copy-start.1) | copy-done | bytes 4194328
  145.6 5.5 %accumulate.4 = (f32[512,768]{1,0:T(8,128)S(1)}, f32[512,768]{1,0:T(8,128)S(1)}) custom-call(s32[2]{0:T(128)S(1)} %pad_add_fusion.1.owners_ref, bf16[4,512,1024]{2,1,0:T(8,128)(2,1)S(1)} %copy-done.1, bf16[4,512,1024]{2,1,0:T(8,128)(2,1)S(1)} %copy-done.1, bf16[4,512,1024]{2,1,0:T(8,128)(2,1)} %collective-permute-done.17.refs_2_.refs_3_.refs_1_.refs_0_, ...), custom_call_target="tpu_custom_call" | custom-call | flops 3221225472 | bytes 13631488 | tf_op jit(solution)/shard_map/accumulate/pallas_call | solution.py:354
  153.4 22.8 %collective-permute-done.16 = bf16[1024,768]{1,0:T(8,128)(2,1)} collective-permute-done((bf16[1024,768]{1,0:T(8,128)(2,1)S(1)}, bf16[1024,768]{1,0:T(8,128)(2,1)}, u32[]{:S(2)}, u32[]{:S(2)}) %collective-permute-start.16) | collective-permute-done | bytes 1572896 | tf_op jit(solution)/shard_map/ppermute | solution.py:138
  183.9 3.3 %accumulate.5 = (f32[512,768]{1,0:T(8,128)S(1)}, f32[512,768]{1,0:T(8,128)S(1)}) custom-call(s32[1]{0:T(128)} %bitcast.10.owners_ref, bf16[4,512,1024]{2,1,0:T(8,128)(2,1)S(1)} %copy-done.2, bf16[4,512,1024]{2,1,0:T(8,128)(2,1)} %collective-permute-done.17.refs_2_.refs_3_.refs_1_.refs_0_, bf16[1024,768]{1,0:T(8,128)(2,1)S(1)} %broadcast_select_fusion.refs_2_, ...), custom_call_target="tpu_custom_call" | custom-call | flops 1610612736 | bytes 9961472 | tf_op jit(solution)/shard_map/accumulate/pallas_call | solution.py:354
  188.4 25.3 %collective-permute-done.19 = bf16[1024,768]{1,0:T(8,128)(2,1)} collective-permute-done((bf16[1024,768]{1,0:T(8,128)(2,1)}, bf16[1024,768]{1,0:T(8,128)(2,1)}, u32[]{:S(2)}, u32[]{:S(2)}) %collective-permute-start.19) | collective-permute-done | bytes 1572896 | tf_op jit(solution)/shard_map/ppermute | solution.py:134
  221.9 6.5 %attention.1 = bf16[512,512]{1,0:T(8,128)(2,1)S(1)} custom-call(f32[512,768]{1,0:T(8,128)S(1)} %accumulate.6.kept_ref, bf16[512,768]{1,0:T(8,128)(2,1)} %collective-permute-done.20.got_ref, f32[512,128]{1,0:T(8,128)S(1)} %get-tuple-element.60.cos_ref, f32[512,128]{1,0:T(8,128)S(1)} %copy-done.13), custom_call_target="tpu_custom_call" | custom-call | flops 536870912 | bytes 3538944 | tf_op jit(solution)/shard_map/attention/pallas_call | solution.py:410
  231.9 6.2 %fetch.1 = (bf16[2048,384]{1,0:T(8,128)(2,1)S(1)}, bf16[2048,3712]{1,0:T(8,128)(2,1)S(1)}) custom-call(bf16[2048,384]{1,0:T(8,128)(2,1)S(1)} %copy-done.8, bf16[2048,3712]{1,0:T(8,128)(2,1)} %all-gather.5.cloned.1.call-done.refs_1_), custom_call_target="tpu_custom_call" | custom-call | bytes 33554432 | tf_op jit(solution)/shard_map/fetch/pallas_call | solution.py:470
  240.3 4.2 %convolution_convert_fusion = bf16[256,3712]{1,0:T(8,128)(2,1)S(1)} fusion(bf16[256,2048]{1,0:T(8,128)(2,1)S(1)} %by_source.1, bf16[2048,3712]{1,0:T(8,128)(2,1)S(1)} %get-tuple-element.69), kind=kOutput, calls=%fused_computation | convolution fusion | flops 3893264384 | bytes 18153472 | tf_op jit(solution)/shard_map/dot_general | solution.py:599
  (106 shorter events, 53.2 us)
Async XLA Ops:
  7.2 73.8 %all-gather.3.cloned.1.call-start = ((), (), s32[]{:S(2)}) async-start(), calls=%async_computation | async-start | bytes 1966080 | tf_op jit(solution)/shard_map/all_gather | solution.py:556
  11.2 220.7 %all-gather.5.cloned.1.call-start = ((), (), s32[]{:S(2)}) async-start(), calls=%async_computation.1 | async-start | bytes 19005440 | tf_op jit(solution)/shard_map/all_gather | solution.py:558
  11.3 17.0 %collective-permute-start = (bf16[2,64,1024]{2,1,0:T(8,128)(2,1)}, bf16[2,64,1024]{2,1,0:T(8,128)(2,1)S(1)}, u32[]{:S(2)}, u32[]{:S(2)}) collective-permute-start(bf16[2,64,1024]{2,1,0:T(8,128)(2,1)} %get-tuple-element.39), channel_id=1, source_target_pairs={{0,8},{4,12},{8,0},{12,4},{16,24},{20,28},{24,16},{28,20},{1,9},{5... | collective-permute-start | bytes 786440 | tf_op jit(solution)/shard_map/ppermute | solution.py:537
  14.4 21.6 %collective-permute-start.1 = (bf16[2,64,1024]{2,1,0:T(8,128)(2,1)}, bf16[2,64,1024]{2,1,0:T(8,128)(2,1)S(1)}, u32[]{:S(2)}, u32[]{:S(2)}) collective-permute-start(bf16[2,64,1024]{2,1,0:T(8,128)(2,1)} %get-tuple-element.40), channel_id=1, source_target_pairs={{0,16},{4,20},{8,24},{12,28},{16,0},{20,4},{24,8},{28,12},{1,17},{... | collective-permute-start | bytes 786440 | tf_op jit(solution)/shard_map/ppermute | solution.py:537
  16.9 19.0 %collective-permute-start.2 = (bf16[2,64,1024]{2,1,0:T(8,128)(2,1)}, bf16[2,64,1024]{2,1,0:T(8,128)(2,1)S(1)}, u32[]{:S(2)}, u32[]{:S(2)}) collective-permute-start(bf16[2,64,1024]{2,1,0:T(8,128)(2,1)} %get-tuple-element.41), channel_id=1, source_target_pairs={{0,24},{4,28},{8,16},{12,20},{16,8},{20,12},{24,0},{28,4},{1,25},{... | collective-permute-start | bytes 786440 | tf_op jit(solution)/shard_map/ppermute | solution.py:537
  36.0 25.4 %collective-permute-start.3 = (bf16[256,1024]{1,0:T(8,128)(2,1)S(1)}, bf16[256,1024]{1,0:T(8,128)(2,1)S(1)}, u32[]{:S(2)}, u32[]{:S(2)}) collective-permute-start(bf16[256,1024]{1,0:T(8,128)(2,1)S(1)} %get-tuple-element.47.refs_0_), channel_id=1, source_target_pairs={{0,1},{1,0},{2,3},{3,2},{4,5},{5,4},{6,7},{7,6},{8,9},{9,8},{10,11... | collective-permute-start | bytes 1572872 | tf_op jit(solution)/shard_map/ppermute | solution.py:191
  37.6 29.4 %collective-permute-start.4 = (bf16[256,1024]{1,0:T(8,128)(2,1)S(1)}, bf16[256,1024]{1,0:T(8,128)(2,1)S(1)}, u32[]{:S(2)}, u32[]{:S(2)}) collective-permute-start(bf16[256,1024]{1,0:T(8,128)(2,1)S(1)} %get-tuple-element.48.refs_1_), channel_id=1, source_target_pairs={{0,1},{1,0},{2,3},{3,2},{4,5},{5,4},{6,7},{7,6},{8,9},{9,8},{10,11... | collective-permute-start | bytes 1572872 | tf_op jit(solution)/shard_map/ppermute | solution.py:191
  38.1 28.8 %collective-permute-start.5 = (bf16[256,1024]{1,0:T(8,128)(2,1)S(1)}, bf16[256,1024]{1,0:T(8,128)(2,1)S(1)}, u32[]{:S(2)}, u32[]{:S(2)}) collective-permute-start(bf16[256,1024]{1,0:T(8,128)(2,1)S(1)} %get-tuple-element.47.refs_0_), channel_id=1, source_target_pairs={{0,2},{1,3},{2,0},{3,1},{4,6},{5,7},{6,4},{7,5},{8,10},{9,11},{10,... | collective-permute-start | bytes 1572872 | tf_op jit(solution)/shard_map/ppermute | solution.py:191
  39.6 27.5 %collective-permute-start.6 = (bf16[256,1024]{1,0:T(8,128)(2,1)S(1)}, bf16[256,1024]{1,0:T(8,128)(2,1)S(1)}, u32[]{:S(2)}, u32[]{:S(2)}) collective-permute-start(bf16[256,1024]{1,0:T(8,128)(2,1)S(1)} %get-tuple-element.48.refs_1_), channel_id=1, source_target_pairs={{0,2},{1,3},{2,0},{3,1},{4,6},{5,7},{6,4},{7,5},{8,10},{9,11},{10,... | collective-permute-start | bytes 1572872 | tf_op jit(solution)/shard_map/ppermute | solution.py:191
  40.1 21.2 %collective-permute-start.7 = (bf16[256,768]{1,0:T(8,128)(2,1)S(1)}, bf16[256,768]{1,0:T(8,128)(2,1)}, u32[]{:S(2)}, u32[]{:S(2)}) collective-permute-start(bf16[256,768]{1,0:T(8,128)(2,1)S(1)} %copy-done.14), channel_id=1, source_target_pairs={{0,16},{4,20},{8,24},{12,28},{16,0},{20,4},{24,8},{28,12},{1,17},{... | collective-permute-start | bytes 1179656 | tf_op jit(solution)/shard_map/ppermute | solution.py:537
  61.4 18.4 %collective-permute-start.10 = (bf16[256,768]{1,0:T(8,128)(2,1)S(1)}, bf16[256,768]{1,0:T(8,128)(2,1)}, u32[]{:S(2)}, u32[]{:S(2)}) collective-permute-start(bf16[256,768]{1,0:T(8,128)(2,1)S(1)} %copy-done.14), channel_id=1, source_target_pairs={{0,8},{4,12},{8,0},{12,4},{16,24},{20,28},{24,16},{28,20},{1,9},{5... | collective-permute-start | bytes 1179656 | tf_op jit(solution)/shard_map/ppermute | solution.py:537
  61.4 18.4 %collective-permute-start.11 = (bf16[256,768]{1,0:T(8,128)(2,1)S(1)}, bf16[256,768]{1,0:T(8,128)(2,1)}, u32[]{:S(2)}, u32[]{:S(2)}) collective-permute-start(bf16[256,768]{1,0:T(8,128)(2,1)S(1)} %copy-done.14), channel_id=1, source_target_pairs={{0,24},{4,28},{8,16},{12,20},{16,8},{20,12},{24,0},{28,4},{1,25},{... | collective-permute-start | bytes 1179656 | tf_op jit(solution)/shard_map/ppermute | solution.py:537
  67.2 12.7 %collective-permute-start.8 = (bf16[256,1024]{1,0:T(8,128)(2,1)S(1)}, bf16[256,1024]{1,0:T(8,128)(2,1)}, u32[]{:S(2)}, u32[]{:S(2)}) collective-permute-start(bf16[256,1024]{1,0:T(8,128)(2,1)S(1)} %collective-permute-done.3.refs_2_), channel_id=1, source_target_pairs={{0,2},{1,3},{2,0},{3,1},{4,6},{5,7},{6,4},{7,5},{8,10},{9,11},{10,... | collective-permute-start | bytes 1572872 | tf_op jit(solution)/shard_map/ppermute | solution.py:191
  68.5 12.5 %collective-permute-start.9 = (bf16[256,1024]{1,0:T(8,128)(2,1)S(1)}, bf16[256,1024]{1,0:T(8,128)(2,1)}, u32[]{:S(2)}, u32[]{:S(2)}) collective-permute-start(bf16[256,1024]{1,0:T(8,128)(2,1)S(1)} %collective-permute-done.6.refs_5_), channel_id=1, source_target_pairs={{0,1},{1,0},{2,3},{3,2},{4,5},{5,4},{6,7},{7,6},{8,9},{9,8},{10,11... | collective-permute-start | bytes 1572872 | tf_op jit(solution)/shard_map/ppermute | solution.py:191
  86.0 56.3 %collective-permute-start.17 = (bf16[4,512,1024]{2,1,0:T(8,128)(2,1)}, bf16[4,512,1024]{2,1,0:T(8,128)(2,1)}, u32[]{:S(2)}, u32[]{:S(2)}) collective-permute-start(bf16[4,512,1024]{2,1,0:T(8,128)(2,1)} %get-tuple-element.55), channel_id=1, source_target_pairs={{0,4},{4,0},{8,12},{12,8},{16,20},{20,16},{24,28},{28,24},{1,5},{5... | collective-permute-start | bytes 12582920 | tf_op jit(solution)/shard_map/ppermute | solution.py:529
  95.5 38.1 %collective-permute-start.13 = (bf16[1024,768]{1,0:T(8,128)(2,1)S(1)}, bf16[1024,768]{1,0:T(8,128)(2,1)}, u32[]{:S(2)}, u32[]{:S(2)}) collective-permute-start(bf16[1024,768]{1,0:T(8,128)(2,1)S(1)} %get-tuple-element.54.refs_4_), channel_id=1, source_target_pairs={{0,8},{4,12},{8,16},{12,20},{16,24},{20,28},{1,9},{5,13},{9,17},{1... | collective-permute-start | bytes 4718600 | tf_op jit(solution)/shard_map/ppermute | solution.py:137
  100.9 38.0 %collective-permute-start.15 = (bf16[1024,768]{1,0:T(8,128)(2,1)S(1)}, bf16[1024,768]{1,0:T(8,128)(2,1)S(1)}, u32[]{:S(2)}, u32[]{:S(2)}) collective-permute-start(bf16[1024,768]{1,0:T(8,128)(2,1)S(1)} %get-tuple-element.54.refs_4_), channel_id=1, source_target_pairs={{8,0},{12,4},{16,8},{20,12},{24,16},{28,20},{9,1},{13,5},{17,9},{2... | collective-permute-start | bytes 4718600 | tf_op jit(solution)/shard_map/ppermute | solution.py:138
  133.6 19.8 %collective-permute-start.14 = (bf16[1024,768]{1,0:T(8,128)(2,1)}, bf16[1024,768]{1,0:T(8,128)(2,1)}, u32[]{:S(2)}, u32[]{:S(2)}) collective-permute-start(bf16[1024,768]{1,0:T(8,128)(2,1)} %collective-permute-done.13), channel_id=1, source_target_pairs={{8,16},{12,20},{16,24},{20,28},{9,17},{13,21},{17,25},{21,29},{10,... | collective-permute-start | bytes 4718600 | tf_op jit(solution)/shard_map/ppermute | solution.py:137
  138.8 37.4 %collective-permute-start.16 = (bf16[1024,768]{1,0:T(8,128)(2,1)S(1)}, bf16[1024,768]{1,0:T(8,128)(2,1)}, u32[]{:S(2)}, u32[]{:S(2)}) collective-permute-start(bf16[1024,768]{1,0:T(8,128)(2,1)S(1)} %collective-permute-done.15), channel_id=1, source_target_pairs={{8,0},{12,4},{16,8},{20,12},{9,1},{13,5},{17,9},{21,13},{10,2},{14... | collective-permute-start | bytes 4718600 | tf_op jit(solution)/shard_map/ppermute | solution.py:138
  176.2 11.0 %collective-permute-start.18 = (bf16[1024,768]{1,0:T(8,128)(2,1)}, bf16[1024,768]{1,0:T(8,128)(2,1)S(1)}, u32[]{:S(2)}, u32[]{:S(2)}) collective-permute-start(bf16[1024,768]{1,0:T(8,128)(2,1)} %collective-permute-done.14), channel_id=1, source_target_pairs={{16,24},{20,28},{17,25},{21,29},{18,26},{22,30},{19,27},{23,31}} | collective-permute-start | bytes 4718600 | tf_op jit(solution)/shard_map/ppermute | solution.py:135
  177.0 36.7 %collective-permute-start.19 = (bf16[1024,768]{1,0:T(8,128)(2,1)}, bf16[1024,768]{1,0:T(8,128)(2,1)}, u32[]{:S(2)}, u32[]{:S(2)}) collective-permute-start(bf16[1024,768]{1,0:T(8,128)(2,1)} %collective-permute-done.16), channel_id=1, source_target_pairs={{8,0},{12,4},{9,1},{13,5},{10,2},{14,6},{11,3},{15,7}} | collective-permute-start | bytes 4718600 | tf_op jit(solution)/shard_map/ppermute | solution.py:134
  228.4 9.8 %collective-permute-start.21 = (bf16[128,512]{1,0:T(8,128)(2,1)S(1)}, bf16[128,512]{1,0:T(8,128)(2,1)S(1)}, u32[]{:S(2)}, u32[]{:S(2)}) collective-permute-start(bf16[128,512]{1,0:T(8,128)(2,1)S(1)} %get-tuple-element.78), channel_id=1, source_target_pairs={{0,1},{1,0},{2,3},{3,2},{4,5},{5,4},{6,7},{7,6},{8,9},{9,8},{10,11... | collective-permute-start | bytes 393224 | tf_op jit(solution)/shard_map/ppermute | solution.py:590
  228.6 9.6 %collective-permute-start.22 = (bf16[128,512]{1,0:T(8,128)(2,1)S(1)}, bf16[128,512]{1,0:T(8,128)(2,1)S(1)}, u32[]{:S(2)}, u32[]{:S(2)}) collective-permute-start(bf16[128,512]{1,0:T(8,128)(2,1)S(1)} %get-tuple-element.77), channel_id=1, source_target_pairs={{0,2},{1,3},{2,0},{3,1},{4,6},{5,7},{6,4},{7,5},{8,10},{9,11},{10,... | collective-permute-start | bytes 393224 | tf_op jit(solution)/shard_map/ppermute | solution.py:590
  229.8 8.4 %collective-permute-start.23 = (bf16[128,512]{1,0:T(8,128)(2,1)S(1)}, bf16[128,512]{1,0:T(8,128)(2,1)S(1)}, u32[]{:S(2)}, u32[]{:S(2)}) collective-permute-start(bf16[128,512]{1,0:T(8,128)(2,1)S(1)} %get-tuple-element.76), channel_id=1, source_target_pairs={{0,3},{1,2},{2,1},{3,0},{4,7},{5,6},{6,5},{7,4},{8,11},{9,10},{10,... | collective-permute-start | bytes 393224 | tf_op jit(solution)/shard_map/ppermute | solution.py:590
  (25 other events, 141.4 us)
Sparse Core Ops, SparseCore 0:
  11.3 40.9 all-gather.2
  81.2 144.0 all-gather.4
where the time goes:
time: 256 us
  waiting for transfers between devices  122 us (48%)
  Pallas kernels  49.3 us (19%)
  starting transfers between devices  35.8 us (14%)
  local copies, waits for them, and re-layouts  22.9 us (9%)
  between operations  14.4 us (6%)
  other arithmetic  6.29 us (2%)
  matrix products  4.94 us (2%)
    ppermute x3, waiting for transfers between devices, hop(): self.high.append(lax.ppermute(down, 'dp', left))  51.6 us
    ppermute x3, waiting for transfers between devices, hop(): self.low.append(lax.ppermute(up, 'dp', right))  31.4 us
    ppermute x6, waiting for transfers between devices, across(): lax.ppermute(block, 'dp', line_pairs([(i, i ^ distance) for i in range(li...  29.5 us
    unnamed x40, local copies, waits for them, and re-layouts  18.5 us
    pallas_call x4, Pallas kernels, accumulate(): pl.pallas_call(kernel, grid_spec=pltpu.PrefetchScalarGridSpec(num_scalar_...  12.9 us
    ppermute x6, starting transfers between devices, across(): lax.ppermute(block, 'dp', line_pairs([(i, i ^ distance) for i in range(li...  12.8 us
    ppermute x3, starting transfers between devices, hop(): self.low.append(lax.ppermute(up, 'dp', right))  7.92 us
    pallas_call x2, Pallas kernels, gradient_term(): pl.pallas_call(kernel, out_shape=jax.ShapeDtypeStruct((size, width), jnp....  7.2 us
  transfers between devices with their start and end apart: 29, of which 14 were waited for; matrix products, arithmetic and copies ran while one was open for 4% of the time, Pallas kernels for 17%

commit v1 on v0

--- a/solution.py
+++ b/solution.py
@@ -362,7 +362,7 @@
             out_specs=[row_spec] * sides,
         ),
         out_shape=[jax.ShapeDtypeStruct((length, width), dtype) for dtype in dtypes],
-        compiler_params=params(20),
+        compiler_params=params(20 if count > 1 else 8 + 4 * sides),
         cost_estimate=pl.CostEstimate(
             flops=2 * sides * count * length * depth * width,
             bytes_accessed=2 * count * depth * (2 * length + width) + 16 * length * width,

time: 256 us -> 256 us (level)
  no operation moved by 1% of the time
where the time goes in v1:
time: 256 us
  waiting for transfers between devices  122 us (48%)
  Pallas kernels  49.3 us (19%)
  starting transfers between devices  35.8 us (14%)
  local copies, waits for them, and re-layouts  22.9 us (9%)
  between operations  14.4 us (6%)
  other arithmetic  6.29 us (2%)
  matrix products  4.94 us (2%)
    ppermute x3, waiting for transfers between devices, hop(): self.high.append(lax.ppermute(down, 'dp', left))  51.6 us
    ppermute x3, waiting for transfers between devices, hop(): self.low.append(lax.ppermute(up, 'dp', right))  31.4 us
    ppermute x6, waiting for transfers between devices, across(): lax.ppermute(block, 'dp', line_pairs([(i, i ^ distance) for i in range(li...  29.5 us
    unnamed x40, local copies, waits for them, and re-layouts  18.5 us
    pallas_call x4, Pallas kernels, accumulate(): pl.pallas_call(kernel, grid_spec=pltpu.PrefetchScalarGridSpec(num_scalar_...  12.9 us
    ppermute x6, starting transfers between devices, across(): lax.ppermute(block, 'dp', line_pairs([(i, i ^ distance) for i in range(li...  12.8 us
    ppermute x3, starting transfers between devices, hop(): self.low.append(lax.ppermute(up, 'dp', right))  7.92 us
    pallas_call x2, Pallas kernels, gradient_term(): pl.pallas_call(kernel, out_shape=jax.ShapeDtypeStruct((size, width), jnp....  7.2 us
  transfers between devices with their start and end apart: 29, of which 14 were waited for; matrix products, arithmetic and copies ran while one was open for 4% of the time, Pallas kernels for 17%

profile of v1, /device:TPU:0, one launch (start us, length us, event | category | flops | bytes accessed | tf_op | source)
XLA Modules:
  0.0 255.7 jit_solution(1265719034556703001)
XLA Ops:
  7.8 3.4 %pack_columns.1 = (bf16[2,64,1024]{2,1,0:T(8,128)(2,1)}, bf16[2,64,1024]{2,1,0:T(8,128)(2,1)}, bf16[2,64,1024]{2,1,0:T(8,128)(2,1)}, bf16[2,64,1024]{2,1,0:T(8,128)(2,1)}, bf16[512,384]{1,0:T(8,128)(2,1)}) custom-call(s32[2]{0:T(128)} %pad_add_fusion.chosen_ref, bf16[256,8192]{1,0:T(8,128)(2,1)} %train_ref.1, bf16[512,8192]{1,0:T(8,128)(2,1)} %refs_2_.1, ...), custom_call_target="tpu_custom_call" | custom-call | tf_op jit(solution)/shard_map/pack_columns/pallas_call | solution.py:70
  11.3 3.1 %collective-permute-start = (bf16[2,64,1024]{2,1,0:T(8,128)(2,1)}, bf16[2,64,1024]{2,1,0:T(8,128)(2,1)S(1)}, u32[]{:S(2)}, u32[]{:S(2)}) collective-permute-start(bf16[2,64,1024]{2,1,0:T(8,128)(2,1)} %get-tuple-element.39), channel_id=1, source_target_pairs={{0,8},{4,12},{8,0},{12,4},{16,24},{20,28},{24,16},{28,20},{1,9},{5... | collective-permute-start | bytes 786440 | tf_op jit(solution)/shard_map/ppermute | solution.py:537
  16.9 3.4 %copy-done.4 = bf16[512,8192]{1,0:T(8,128)(2,1)S(1)} copy-done((bf16[512,8192]{1,0:T(8,128)(2,1)S(1)}, bf16[512,8192]{1,0:T(8,128)(2,1)}, u32[]{:S(2)}) %copy-start.4) | copy-done | bytes 8388632
  20.3 6.0 %norm_columns.1 = (bf16[4,512,1024]{2,1,0:T(8,128)(2,1)S(1)}, bf16[4,512,1024]{2,1,0:T(8,128)(2,1)}) custom-call(bf16[512,8192]{1,0:T(8,128)(2,1)S(1)} %copy-done.4, f32[1,8192]{1,0:T(1,128)S(1)} %bitcast.24), custom_call_target="tpu_custom_call" | custom-call | flops 25165824 | bytes 16777216 | tf_op jit(solution)/shard_map/norm_columns/pallas_call | solution.py:310
  28.3 7.7 %collective-permute-done.1.refs_2_ = bf16[2,64,1024]{2,1,0:T(8,128)(2,1)S(1)} collective-permute-done((bf16[2,64,1024]{2,1,0:T(8,128)(2,1)}, bf16[2,64,1024]{2,1,0:T(8,128)(2,1)S(1)}, u32[]{:S(2)}, u32[]{:S(2)}) %collective-permute-start.1) | collective-permute-done | bytes 262176 | tf_op jit(solution)/shard_map/ppermute | solution.py:537
  40.1 5.8 %collective-permute-start.7 = (bf16[256,768]{1,0:T(8,128)(2,1)S(1)}, bf16[256,768]{1,0:T(8,128)(2,1)}, u32[]{:S(2)}, u32[]{:S(2)}) collective-permute-start(bf16[256,768]{1,0:T(8,128)(2,1)S(1)} %copy-done.14), channel_id=1, source_target_pairs={{0,16},{4,20},{8,24},{12,28},{16,0},{20,4},{24,8},{28,12},{1,17},{... | collective-permute-start | bytes 1179656 | tf_op jit(solution)/shard_map/ppermute | solution.py:537
  45.9 15.5 %collective-permute-done.7 = bf16[256,768]{1,0:T(8,128)(2,1)} collective-permute-done((bf16[256,768]{1,0:T(8,128)(2,1)S(1)}, bf16[256,768]{1,0:T(8,128)(2,1)}, u32[]{:S(2)}, u32[]{:S(2)}) %collective-permute-start.7) | collective-permute-done | bytes 393248 | tf_op jit(solution)/shard_map/ppermute | solution.py:537
  62.7 4.2 %collective-permute-done.4.refs_3_ = bf16[256,1024]{1,0:T(8,128)(2,1)S(1)} collective-permute-done((bf16[256,1024]{1,0:T(8,128)(2,1)S(1)}, bf16[256,1024]{1,0:T(8,128)(2,1)S(1)}, u32[]{:S(2)}, u32[]{:S(2)}) %collective-permute-start.4) | collective-permute-done | bytes 524320 | tf_op jit(solution)/shard_map/ppermute | solution.py:191
  69.2 4.2 %constant_dynamic-slice_fusion = bf16[512,3712]{1,0:T(8,128)(2,1)} fusion(bf16[512,8192]{1,0:T(8,128)(2,1)} %refs_2_.1, s32[]{:T(128)S(6)} %select_n.76), kind=kLoop, calls=%fused_computation.11 | loop fusion | bytes 7602180 | tf_op jit(solution)/shard_map/dynamic_slice | solution.py:551
  73.4 6.4 %collective-permute-done.10 = bf16[256,768]{1,0:T(8,128)(2,1)} collective-permute-done((bf16[256,768]{1,0:T(8,128)(2,1)S(1)}, bf16[256,768]{1,0:T(8,128)(2,1)}, u32[]{:S(2)}, u32[]{:S(2)}) %collective-permute-start.10) | collective-permute-done | bytes 393248 | tf_op jit(solution)/shard_map/ppermute | solution.py:537
  82.4 3.5 %gradient_term.3 = bf16[1024,768]{1,0:T(8,128)(2,1)S(1)} custom-call(bf16[256,1024]{1,0:T(8,128)(2,1)S(1)} %get-tuple-element.47.refs_0_, bf16[256,1024]{1,0:T(8,128)(2,1)S(1)} %get-tuple-element.48.refs_1_, bf16[256,1024]{1,0:T(8,128)(2,1)S(1)} %collective-permute-done.3.refs_2_, bf16[256,1024]{1,0:T(8,128)(2,1)S(1)} %collective-permute-done.4.refs_3_, ...), custom_call_target="tpu_custom_call" | custom-call | flops 1610612736 | bytes 8912896 | tf_op jit(solution)/shard_map/gradient_term/pallas_call | solution.py:243
  86.5 3.7 %gradient_term.2.kept_ref = f32[1024,768]{1,0:T(8,128)S(1)} custom-call(bf16[256,1024]{1,0:T(8,128)(2,1)S(1)} %get-tuple-element.47.refs_0_, bf16[256,1024]{1,0:T(8,128)(2,1)S(1)} %get-tuple-element.48.refs_1_, bf16[256,1024]{1,0:T(8,128)(2,1)S(1)} %collective-permute-done.3.refs_2_, bf16[256,1024]{1,0:T(8,128)(2,1)S(1)} %collective-permute-done.4.refs_3_, ...), custom_call_target="tpu_custom_call" | custom-call | flops 1610612736 | bytes 8912896 | tf_op jit(solution)/shard_map/gradient_term/pallas_call | solution.py:243
  91.3 4.2 %adam_rows.1 = (f32[1024,768]{1,0:T(8,128)}, bf16[1024,768]{1,0:T(8,128)(2,1)S(1)}) custom-call(f32[1024,768]{1,0:T(8,128)S(1)} %gradient_term.2.kept_ref, bf16[1024,768]{1,0:T(8,128)(2,1)S(1)} %collective-permute-done.12.got_ref, f32[1024,768]{1,0:T(8,128)S(1)} %copy-done.5, f32[1024,768]{1,0:T(8,128)S(1)} %copy-done.6, f32[1024,768]{1,0:T(8,128)S(1)} %copy-done.7), custom_call_target="tpu_custom_call" | custom-call | flops 12582912 | bytes 18874368 | tf_op jit(solution)/shard_map/adam_rows/pallas_call | solution.py:272
  95.5 5.4 %collective-permute-start.13 = (bf16[1024,768]{1,0:T(8,128)(2,1)S(1)}, bf16[1024,768]{1,0:T(8,128)(2,1)}, u32[]{:S(2)}, u32[]{:S(2)}) collective-permute-start(bf16[1024,768]{1,0:T(8,128)(2,1)S(1)} %get-tuple-element.54.refs_4_), channel_id=1, source_target_pairs={{0,8},{4,12},{8,16},{12,20},{16,24},{20,28},{1,9},{5,13},{9,17},{1... | collective-permute-start | bytes 4718600 | tf_op jit(solution)/shard_map/ppermute | solution.py:137
  102.1 31.4 %collective-permute-done.13 = bf16[1024,768]{1,0:T(8,128)(2,1)} collective-permute-done((bf16[1024,768]{1,0:T(8,128)(2,1)S(1)}, bf16[1024,768]{1,0:T(8,128)(2,1)}, u32[]{:S(2)}, u32[]{:S(2)}) %collective-permute-start.13) | collective-permute-done | bytes 1572896 | tf_op jit(solution)/shard_map/ppermute | solution.py:137
  135.4 3.4 %collective-permute-done.15 = bf16[1024,768]{1,0:T(8,128)(2,1)S(1)} collective-permute-done((bf16[1024,768]{1,0:T(8,128)(2,1)S(1)}, bf16[1024,768]{1,0:T(8,128)(2,1)S(1)}, u32[]{:S(2)}, u32[]{:S(2)}) %collective-permute-start.15) | collective-permute-done | bytes 1572896 | tf_op jit(solution)/shard_map/ppermute | solution.py:138
  142.3 3.3 %copy-done.1 = bf16[4,512,1024]{2,1,0:T(8,128)(2,1)S(1)} copy-done((bf16[4,512,1024]{2,1,0:T(8,128)(2,1)S(1)}, bf16[4,512,1024]{2,1,0:T(8,128)(2,1)}, u32[]{:S(2)}) %copy-start.1) | copy-done | bytes 4194328
  145.6 5.5 %accumulate.4 = (f32[512,768]{1,0:T(8,128)S(1)}, f32[512,768]{1,0:T(8,128)S(1)}) custom-call(s32[2]{0:T(128)S(1)} %pad_add_fusion.1.owners_ref, bf16[4,512,1024]{2,1,0:T(8,128)(2,1)S(1)} %copy-done.1, bf16[4,512,1024]{2,1,0:T(8,128)(2,1)S(1)} %copy-done.1, bf16[4,512,1024]{2,1,0:T(8,128)(2,1)} %collective-permute-done.17.refs_2_.refs_3_.refs_1_.refs_0_, ...), custom_call_target="tpu_custom_call" | custom-call | flops 3221225472 | bytes 13631488 | tf_op jit(solution)/shard_map/accumulate/pallas_call | solution.py:354
  153.4 22.8 %collective-permute-done.16 = bf16[1024,768]{1,0:T(8,128)(2,1)} collective-permute-done((bf16[1024,768]{1,0:T(8,128)(2,1)S(1)}, bf16[1024,768]{1,0:T(8,128)(2,1)}, u32[]{:S(2)}, u32[]{:S(2)}) %collective-permute-start.16) | collective-permute-done | bytes 1572896 | tf_op jit(solution)/shard_map/ppermute | solution.py:138
  183.9 3.3 %accumulate.5 = (f32[512,768]{1,0:T(8,128)S(1)}, f32[512,768]{1,0:T(8,128)S(1)}) custom-call(s32[1]{0:T(128)} %bitcast.10.owners_ref, bf16[4,512,1024]{2,1,0:T(8,128)(2,1)S(1)} %copy-done.2, bf16[4,512,1024]{2,1,0:T(8,128)(2,1)} %collective-permute-done.17.refs_2_.refs_3_.refs_1_.refs_0_, bf16[1024,768]{1,0:T(8,128)(2,1)S(1)} %broadcast_select_fusion.refs_2_, ...), custom_call_target="tpu_custom_call" | custom-call | flops 1610612736 | bytes 9961472 | tf_op jit(solution)/shard_map/accumulate/pallas_call | solution.py:354
  188.4 25.3 %collective-permute-done.19 = bf16[1024,768]{1,0:T(8,128)(2,1)} collective-permute-done((bf16[1024,768]{1,0:T(8,128)(2,1)}, bf16[1024,768]{1,0:T(8,128)(2,1)}, u32[]{:S(2)}, u32[]{:S(2)}) %collective-permute-start.19) | collective-permute-done | bytes 1572896 | tf_op jit(solution)/shard_map/ppermute | solution.py:134
  221.9 6.5 %attention.1 = bf16[512,512]{1,0:T(8,128)(2,1)S(1)} custom-call(f32[512,768]{1,0:T(8,128)S(1)} %accumulate.6.kept_ref, bf16[512,768]{1,0:T(8,128)(2,1)} %collective-permute-done.20.got_ref, f32[512,128]{1,0:T(8,128)S(1)} %get-tuple-element.60.cos_ref, f32[512,128]{1,0:T(8,128)S(1)} %copy-done.13), custom_call_target="tpu_custom_call" | custom-call | flops 536870912 | bytes 3538944 | tf_op jit(solution)/shard_map/attention/pallas_call | solution.py:410
  231.9 6.2 %fetch.1 = (bf16[2048,384]{1,0:T(8,128)(2,1)S(1)}, bf16[2048,3712]{1,0:T(8,128)(2,1)S(1)}) custom-call(bf16[2048,384]{1,0:T(8,128)(2,1)S(1)} %copy-done.8, bf16[2048,3712]{1,0:T(8,128)(2,1)} %all-gather.5.cloned.1.call-done.refs_1_), custom_call_target="tpu_custom_call" | custom-call | bytes 33554432 | tf_op jit(solution)/shard_map/fetch/pallas_call | solution.py:470
  240.3 4.2 %convolution_convert_fusion = bf16[256,3712]{1,0:T(8,128)(2,1)S(1)} fusion(bf16[256,2048]{1,0:T(8,128)(2,1)S(1)} %by_source.1, bf16[2048,3712]{1,0:T(8,128)(2,1)S(1)} %get-tuple-element.69), kind=kOutput, calls=%fused_computation | convolution fusion | flops 3893264384 | bytes 18153472 | tf_op jit(solution)/shard_map/dot_general | solution.py:599
  (106 shorter events, 53.2 us)
Async XLA Ops:
  7.2 73.8 %all-gather.3.cloned.1.call-start = ((), (), s32[]{:S(2)}) async-start(), calls=%async_computation | async-start | bytes 1966080 | tf_op jit(solution)/shard_map/all_gather | solution.py:556
  11.2 220.7 %all-gather.5.cloned.1.call-start = ((), (), s32[]{:S(2)}) async-start(), calls=%async_computation.1 | async-start | bytes 19005440 | tf_op jit(solution)/shard_map/all_gather | solution.py:558
  11.3 17.0 %collective-permute-start = (bf16[2,64,1024]{2,1,0:T(8,128)(2,1)}, bf16[2,64,1024]{2,1,0:T(8,128)(2,1)S(1)}, u32[]{:S(2)}, u32[]{:S(2)}) collective-permute-start(bf16[2,64,1024]{2,1,0:T(8,128)(2,1)} %get-tuple-element.39), channel_id=1, source_target_pairs={{0,8},{4,12},{8,0},{12,4},{16,24},{20,28},{24,16},{28,20},{1,9},{5... | collective-permute-start | bytes 786440 | tf_op jit(solution)/shard_map/ppermute | solution.py:537
  14.4 21.6 %collective-permute-start.1 = (bf16[2,64,1024]{2,1,0:T(8,128)(2,1)}, bf16[2,64,1024]{2,1,0:T(8,128)(2,1)S(1)}, u32[]{:S(2)}, u32[]{:S(2)}) collective-permute-start(bf16[2,64,1024]{2,1,0:T(8,128)(2,1)} %get-tuple-element.40), channel_id=1, source_target_pairs={{0,16},{4,20},{8,24},{12,28},{16,0},{20,4},{24,8},{28,12},{1,17},{... | collective-permute-start | bytes 786440 | tf_op jit(solution)/shard_map/ppermute | solution.py:537
  16.9 19.0 %collective-permute-start.2 = (bf16[2,64,1024]{2,1,0:T(8,128)(2,1)}, bf16[2,64,1024]{2,1,0:T(8,128)(2,1)S(1)}, u32[]{:S(2)}, u32[]{:S(2)}) collective-permute-start(bf16[2,64,1024]{2,1,0:T(8,128)(2,1)} %get-tuple-element.41), channel_id=1, source_target_pairs={{0,24},{4,28},{8,16},{12,20},{16,8},{20,12},{24,0},{28,4},{1,25},{... | collective-permute-start | bytes 786440 | tf_op jit(solution)/shard_map/ppermute | solution.py:537
  36.0 25.4 %collective-permute-start.3 = (bf16[256,1024]{1,0:T(8,128)(2,1)S(1)}, bf16[256,1024]{1,0:T(8,128)(2,1)S(1)}, u32[]{:S(2)}, u32[]{:S(2)}) collective-permute-start(bf16[256,1024]{1,0:T(8,128)(2,1)S(1)} %get-tuple-element.47.refs_0_), channel_id=1, source_target_pairs={{0,1},{1,0},{2,3},{3,2},{4,5},{5,4},{6,7},{7,6},{8,9},{9,8},{10,11... | collective-permute-start | bytes 1572872 | tf_op jit(solution)/shard_map/ppermute | solution.py:191
  37.6 29.4 %collective-permute-start.4 = (bf16[256,1024]{1,0:T(8,128)(2,1)S(1)}, bf16[256,1024]{1,0:T(8,128)(2,1)S(1)}, u32[]{:S(2)}, u32[]{:S(2)}) collective-permute-start(bf16[256,1024]{1,0:T(8,128)(2,1)S(1)} %get-tuple-element.48.refs_1_), channel_id=1, source_target_pairs={{0,1},{1,0},{2,3},{3,2},{4,5},{5,4},{6,7},{7,6},{8,9},{9,8},{10,11... | collective-permute-start | bytes 1572872 | tf_op jit(solution)/shard_map/ppermute | solution.py:191
  38.1 28.8 %collective-permute-start.5 = (bf16[256,1024]{1,0:T(8,128)(2,1)S(1)}, bf16[256,1024]{1,0:T(8,128)(2,1)S(1)}, u32[]{:S(2)}, u32[]{:S(2)}) collective-permute-start(bf16[256,1024]{1,0:T(8,128)(2,1)S(1)} %get-tuple-element.47.refs_0_), channel_id=1, source_target_pairs={{0,2},{1,3},{2,0},{3,1},{4,6},{5,7},{6,4},{7,5},{8,10},{9,11},{10,... | collective-permute-start | bytes 1572872 | tf_op jit(solution)/shard_map/ppermute | solution.py:191
  39.6 27.5 %collective-permute-start.6 = (bf16[256,1024]{1,0:T(8,128)(2,1)S(1)}, bf16[256,1024]{1,0:T(8,128)(2,1)S(1)}, u32[]{:S(2)}, u32[]{:S(2)}) collective-permute-start(bf16[256,1024]{1,0:T(8,128)(2,1)S(1)} %get-tuple-element.48.refs_1_), channel_id=1, source_target_pairs={{0,2},{1,3},{2,0},{3,1},{4,6},{5,7},{6,4},{7,5},{8,10},{9,11},{10,... | collective-permute-start | bytes 1572872 | tf_op jit(solution)/shard_map/ppermute | solution.py:191
  40.1 21.2 %collective-permute-start.7 = (bf16[256,768]{1,0:T(8,128)(2,1)S(1)}, bf16[256,768]{1,0:T(8,128)(2,1)}, u32[]{:S(2)}, u32[]{:S(2)}) collective-permute-start(bf16[256,768]{1,0:T(8,128)(2,1)S(1)} %copy-done.14), channel_id=1, source_target_pairs={{0,16},{4,20},{8,24},{12,28},{16,0},{20,4},{24,8},{28,12},{1,17},{... | collective-permute-start | bytes 1179656 | tf_op jit(solution)/shard_map/ppermute | solution.py:537
  61.4 18.4 %collective-permute-start.10 = (bf16[256,768]{1,0:T(8,128)(2,1)S(1)}, bf16[256,768]{1,0:T(8,128)(2,1)}, u32[]{:S(2)}, u32[]{:S(2)}) collective-permute-start(bf16[256,768]{1,0:T(8,128)(2,1)S(1)} %copy-done.14), channel_id=1, source_target_pairs={{0,8},{4,12},{8,0},{12,4},{16,24},{20,28},{24,16},{28,20},{1,9},{5... | collective-permute-start | bytes 1179656 | tf_op jit(solution)/shard_map/ppermute | solution.py:537
  61.4 18.4 %collective-permute-start.11 = (bf16[256,768]{1,0:T(8,128)(2,1)S(1)}, bf16[256,768]{1,0:T(8,128)(2,1)}, u32[]{:S(2)}, u32[]{:S(2)}) collective-permute-start(bf16[256,768]{1,0:T(8,128)(2,1)S(1)} %copy-done.14), channel_id=1, source_target_pairs={{0,24},{4,28},{8,16},{12,20},{16,8},{20,12},{24,0},{28,4},{1,25},{... | collective-permute-start | bytes 1179656 | tf_op jit(solution)/shard_map/ppermute | solution.py:537
  67.2 12.7 %collective-permute-start.8 = (bf16[256,1024]{1,0:T(8,128)(2,1)S(1)}, bf16[256,1024]{1,0:T(8,128)(2,1)}, u32[]{:S(2)}, u32[]{:S(2)}) collective-permute-start(bf16[256,1024]{1,0:T(8,128)(2,1)S(1)} %collective-permute-done.3.refs_2_), channel_id=1, source_target_pairs={{0,2},{1,3},{2,0},{3,1},{4,6},{5,7},{6,4},{7,5},{8,10},{9,11},{10,... | collective-permute-start | bytes 1572872 | tf_op jit(solution)/shard_map/ppermute | solution.py:191
  68.5 12.5 %collective-permute-start.9 = (bf16[256,1024]{1,0:T(8,128)(2,1)S(1)}, bf16[256,1024]{1,0:T(8,128)(2,1)}, u32[]{:S(2)}, u32[]{:S(2)}) collective-permute-start(bf16[256,1024]{1,0:T(8,128)(2,1)S(1)} %collective-permute-done.6.refs_5_), channel_id=1, source_target_pairs={{0,1},{1,0},{2,3},{3,2},{4,5},{5,4},{6,7},{7,6},{8,9},{9,8},{10,11... | collective-permute-start | bytes 1572872 | tf_op jit(solution)/shard_map/ppermute | solution.py:191
  86.0 56.3 %collective-permute-start.17 = (bf16[4,512,1024]{2,1,0:T(8,128)(2,1)}, bf16[4,512,1024]{2,1,0:T(8,128)(2,1)}, u32[]{:S(2)}, u32[]{:S(2)}) collective-permute-start(bf16[4,512,1024]{2,1,0:T(8,128)(2,1)} %get-tuple-element.55), channel_id=1, source_target_pairs={{0,4},{4,0},{8,12},{12,8},{16,20},{20,16},{24,28},{28,24},{1,5},{5... | collective-permute-start | bytes 12582920 | tf_op jit(solution)/shard_map/ppermute | solution.py:529
  95.5 38.1 %collective-permute-start.13 = (bf16[1024,768]{1,0:T(8,128)(2,1)S(1)}, bf16[1024,768]{1,0:T(8,128)(2,1)}, u32[]{:S(2)}, u32[]{:S(2)}) collective-permute-start(bf16[1024,768]{1,0:T(8,128)(2,1)S(1)} %get-tuple-element.54.refs_4_), channel_id=1, source_target_pairs={{0,8},{4,12},{8,16},{12,20},{16,24},{20,28},{1,9},{5,13},{9,17},{1... | collective-permute-start | bytes 4718600 | tf_op jit(solution)/shard_map/ppermute | solution.py:137
  100.9 38.0 %collective-permute-start.15 = (bf16[1024,768]{1,0:T(8,128)(2,1)S(1)}, bf16[1024,768]{1,0:T(8,128)(2,1)S(1)}, u32[]{:S(2)}, u32[]{:S(2)}) collective-permute-start(bf16[1024,768]{1,0:T(8,128)(2,1)S(1)} %get-tuple-element.54.refs_4_), channel_id=1, source_target_pairs={{8,0},{12,4},{16,8},{20,12},{24,16},{28,20},{9,1},{13,5},{17,9},{2... | collective-permute-start | bytes 4718600 | tf_op jit(solution)/shard_map/ppermute | solution.py:138
  133.6 19.8 %collective-permute-start.14 = (bf16[1024,768]{1,0:T(8,128)(2,1)}, bf16[1024,768]{1,0:T(8,128)(2,1)}, u32[]{:S(2)}, u32[]{:S(2)}) collective-permute-start(bf16[1024,768]{1,0:T(8,128)(2,1)} %collective-permute-done.13), channel_id=1, source_target_pairs={{8,16},{12,20},{16,24},{20,28},{9,17},{13,21},{17,25},{21,29},{10,... | collective-permute-start | bytes 4718600 | tf_op jit(solution)/shard_map/ppermute | solution.py:137
  138.8 37.4 %collective-permute-start.16 = (bf16[1024,768]{1,0:T(8,128)(2,1)S(1)}, bf16[1024,768]{1,0:T(8,128)(2,1)}, u32[]{:S(2)}, u32[]{:S(2)}) collective-permute-start(bf16[1024,768]{1,0:T(8,128)(2,1)S(1)} %collective-permute-done.15), channel_id=1, source_target_pairs={{8,0},{12,4},{16,8},{20,12},{9,1},{13,5},{17,9},{21,13},{10,2},{14... | collective-permute-start | bytes 4718600 | tf_op jit(solution)/shard_map/ppermute | solution.py:138
  176.2 11.0 %collective-permute-start.18 = (bf16[1024,768]{1,0:T(8,128)(2,1)}, bf16[1024,768]{1,0:T(8,128)(2,1)S(1)}, u32[]{:S(2)}, u32[]{:S(2)}) collective-permute-start(bf16[1024,768]{1,0:T(8,128)(2,1)} %collective-permute-done.14), channel_id=1, source_target_pairs={{16,24},{20,28},{17,25},{21,29},{18,26},{22,30},{19,27},{23,31}} | collective-permute-start | bytes 4718600 | tf_op jit(solution)/shard_map/ppermute | solution.py:135
  177.0 36.7 %collective-permute-start.19 = (bf16[1024,768]{1,0:T(8,128)(2,1)}, bf16[1024,768]{1,0:T(8,128)(2,1)}, u32[]{:S(2)}, u32[]{:S(2)}) collective-permute-start(bf16[1024,768]{1,0:T(8,128)(2,1)} %collective-permute-done.16), channel_id=1, source_target_pairs={{8,0},{12,4},{9,1},{13,5},{10,2},{14,6},{11,3},{15,7}} | collective-permute-start | bytes 4718600 | tf_op jit(solution)/shard_map/ppermute | solution.py:134
  228.4 9.8 %collective-permute-start.21 = (bf16[128,512]{1,0:T(8,128)(2,1)S(1)}, bf16[128,512]{1,0:T(8,128)(2,1)S(1)}, u32[]{:S(2)}, u32[]{:S(2)}) collective-permute-start(bf16[128,512]{1,0:T(8,128)(2,1)S(1)} %get-tuple-element.78), channel_id=1, source_target_pairs={{0,1},{1,0},{2,3},{3,2},{4,5},{5,4},{6,7},{7,6},{8,9},{9,8},{10,11... | collective-permute-start | bytes 393224 | tf_op jit(solution)/shard_map/ppermute | solution.py:590
  228.6 9.6 %collective-permute-start.22 = (bf16[128,512]{1,0:T(8,128)(2,1)S(1)}, bf16[128,512]{1,0:T(8,128)(2,1)S(1)}, u32[]{:S(2)}, u32[]{:S(2)}) collective-permute-start(bf16[128,512]{1,0:T(8,128)(2,1)S(1)} %get-tuple-element.77), channel_id=1, source_target_pairs={{0,2},{1,3},{2,0},{3,1},{4,6},{5,7},{6,4},{7,5},{8,10},{9,11},{10,... | collective-permute-start | bytes 393224 | tf_op jit(solution)/shard_map/ppermute | solution.py:590
  229.8 8.4 %collective-permute-start.23 = (bf16[128,512]{1,0:T(8,128)(2,1)S(1)}, bf16[128,512]{1,0:T(8,128)(2,1)S(1)}, u32[]{:S(2)}, u32[]{:S(2)}) collective-permute-start(bf16[128,512]{1,0:T(8,128)(2,1)S(1)} %get-tuple-element.76), channel_id=1, source_target_pairs={{0,3},{1,2},{2,1},{3,0},{4,7},{5,6},{6,5},{7,4},{8,11},{9,10},{10,... | collective-permute-start | bytes 393224 | tf_op jit(solution)/shard_map/ppermute | solution.py:590
  (25 other events, 141.4 us)
Sparse Core Ops, SparseCore 0:
  11.3 40.9 all-gather.2
  81.2 144.0 all-gather.4
